TPU v7x, 32 devices: a whole 2x2x4 slice. The times are simulated.
32 devices in a mesh: group: 4 (over z), tensor: 8 (over y, x, core).
Axes of the slice: x: 2, y: 2, z: 4, core: 2. Of those that a mesh axis runs over, the one named last changes fastest.
Arguments:
- residual_in: bfloat16 [1024, 2048], P(('group', 'tensor')), parts along dimension 0, may hold values from -22 to 22
- attn_gain: float32 [2048], replicated, may hold values from 0.5 to 1.5
- w_query: bfloat16 [2048, 4096], P(None, 'tensor'), may hold values from -0.125 to 0.125
- w_keyval: bfloat16 [1024, 2048], P('tensor'), may hold values from -0.125 to 0.125
- query_gain: float32 [128], replicated, may hold values from 0.1 to 1.9
- key_gain: float32 [128], replicated, may hold values from 0.1 to 1.9
- w_out: bfloat16 [4096, 2048], P('tensor'), may hold values from -0.09375 to 0.09375
- ffn_gain: float32 [2048], replicated, may hold values from 0.5 to 1.5
- w_gate: bfloat16 [8, 768, 2048], P('tensor'), may hold values from -0.125 to 0.125
- w_up: bfloat16 [8, 768, 2048], P('tensor'), may hold values from -0.125 to 0.125
- w_down: bfloat16 [8, 768, 2048], P('tensor'), may hold values from -0.21875 to 0.21875
- key_cache: bfloat16 [32, 1024, 512], P(('group', 'tensor')), parts along dimension 0, may hold values from -110 to 110
- value_cache: bfloat16 [32, 1024, 512], P(('group', 'tensor')), parts along dimension 0, may hold values from -18 to 18
- prefix_lens: int32 [32], P(('group', 'tensor')), parts along dimension 0, may hold values from 1 to 992
- accepted: int32 [32], P(('group', 'tensor')), parts along dimension 0, may hold values from 1 to 8
- accept_path: int32 [32, 8], P(('group', 'tensor')), parts along dimension 0, may hold values from 0 to 14, as said below
- parents: int32 [32, 32], P(('group', 'tensor')), parts along dimension 0, may hold values from -1 to 30, as said below
- slot_kinds: int32 [32], P(('group', 'tensor')), parts along dimension 0, may hold values from 0 to 1
- expert_ids: int32 [1024, 8], P('group'), parts along dimension 0, may hold values from 0 to 127, as said below
- gate_probs: float32 [1024, 8], P('group'), parts along dimension 0, may hold values from 0.1 to 1
Outputs:
- mixed: bfloat16 [1024, 2048], P(('group', 'tensor')), parts along dimension 0
There are 4 independent parts, one for each index of `group`. A program takes and returns all parts, laid end to end along the dimension named above; an argument that names none is the same for every part. Nothing has to cross between parts.
Inputs may be any that keep to these rules, and one draw needn't show every extreme that they name: `expert_ids`: the tokens of each slot name each of the 128 experts exactly 32 * 8 // 128 times; a token never names one expert twice. `accept_path`: each row starts at 0 and rises by 1 or 2 from one entry to the next. `parents`: node 0 of every slot has parent -1; every other node's parent is an earlier node of the same slot.
All inputs are finite; a program needn't handle non-finite values.
Results may differ from a plain program's by a relative error of at most 0.02.
Values may be sent and summed in bfloat16 or wider, within the bound.
No kernel may reach another device: no remote copies, remote signals or barrier semaphores. Data moves between devices by JAX's collectives and lax.ppermute only.
A program may use at most 128 MiB of HBM per device.

v0:
```python
import math

import jax
import jax.numpy as jnp
from jax import lax
from jax.sharding import PartitionSpec as P

EXPERTS = 128
SINK = 4
WIN = 512


EPSILON = 1e-06
NEG_FILL = -1e30
ROPE_BASE = 1000000.0


def rms_rows(values, weight_gain):
    return (
        values
        * lax.rsqrt(jnp.mean(values * values, axis=-1, keepdims=True) + EPSILON)
        * weight_gain
    )


def rotate(values, angles):
    half_dim = values.shape[-1] // 2
    cosine = jnp.cos(angles)[:, None, :]
    sine_val = jnp.sin(angles)[:, None, :]
    lower_half = values[..., :half_dim]
    upper_half = values[..., half_dim:]
    return jnp.concatenate(
        [lower_half * cosine - upper_half * sine_val, upper_half * cosine + lower_half * sine_val],
        axis=-1,
    )


def ancestors(parent_row, count_new):
    parent_link = jax.nn.one_hot(parent_row, count_new, dtype=jnp.float32)
    reach_mat = jnp.eye(count_new, dtype=jnp.float32) + parent_link
    for unused in range((count_new - 1).bit_length()):
        reach_mat = jnp.minimum(jnp.dot(reach_mat, reach_mat, precision=lax.Precision.HIGHEST), 1.0)
    return reach_mat


def attend_parts(
    query_raw,
    keyval_raw,
    key_cache,
    value_cache,
    prefix_len,
    accepted_len,
    path_row,
    parent_row,
    kind_value,
    query_gain,
    key_gain,
):
    count_new = query_raw.shape[0]
    head_dim = query_gain.shape[0]
    kv_heads = key_cache.shape[-1] // head_dim
    q_heads = query_raw.shape[-1] // head_dim
    group_size = q_heads // kv_heads
    cache_len = key_cache.shape[0]
    acc_count = path_row.shape[0]
    total_len = prefix_len + accepted_len
    reach_mat = ancestors(parent_row, count_new)
    index_row = jnp.arange(count_new)
    causal = (index_row[None, :] <= index_row[:, None]).astype(jnp.float32)
    is_tree = kind_value == 1
    allowed = jnp.where(is_tree, reach_mat, causal) > 0.5
    depth_used = jnp.where(is_tree, jnp.sum(reach_mat, axis=1) - 1.0, index_row.astype(jnp.float32))
    position = total_len.astype(jnp.float32) + depth_used
    half_dim = head_dim // 2
    freq_table = jnp.exp(
        -(2.0 * jnp.arange(half_dim, dtype=jnp.float32) / head_dim) * math.log(ROPE_BASE)
    )
    angles = position[:, None] * freq_table[None, :]
    query_rot = rotate(
        rms_rows(query_raw.astype(jnp.float32).reshape(count_new, q_heads, head_dim), query_gain),
        angles,
    ).astype(jnp.bfloat16)
    key_width = kv_heads * head_dim
    key_new = rotate(
        rms_rows(
            keyval_raw[:, :key_width].astype(jnp.float32).reshape(count_new, kv_heads, head_dim),
            key_gain,
        ),
        angles,
    ).astype(jnp.bfloat16)
    value_new = keyval_raw[:, key_width:].reshape(count_new, kv_heads, head_dim)
    acc_rows = prefix_len + path_row
    key_acc = jnp.take(key_cache, acc_rows, axis=0).reshape(acc_count, kv_heads, head_dim)
    value_acc = jnp.take(value_cache, acc_rows, axis=0).reshape(acc_count, kv_heads, head_dim)
    key_old = key_cache.reshape(cache_len, kv_heads, head_dim)
    value_old = value_cache.reshape(cache_len, kv_heads, head_dim)
    cache_pos = jnp.arange(cache_len)
    seen_old = (cache_pos < prefix_len) & ((cache_pos < SINK) | (cache_pos >= total_len - WIN))
    acc_index = jnp.arange(acc_count)
    acc_pos = prefix_len + acc_index
    seen_acc = (acc_index < accepted_len) & ((acc_pos < SINK) | (acc_pos >= total_len - WIN))
    score_scale = head_dim ** (-0.5)
    query_group = query_rot.reshape(count_new, kv_heads, group_size, head_dim)
    score_old = (
        jnp.einsum("nkgd,mkd->kgnm", query_group, key_old, preferred_element_type=jnp.float32)
        * score_scale
    )
    score_acc = (
        jnp.einsum("nkgd,mkd->kgnm", query_group, key_acc, preferred_element_type=jnp.float32)
        * score_scale
    )
    score_new = (
        jnp.einsum("nkgd,mkd->kgnm", query_group, key_new, preferred_element_type=jnp.float32)
        * score_scale
    )
    score_old = jnp.where(seen_old[None, None, None, :], score_old, NEG_FILL)
    score_acc = jnp.where(seen_acc[None, None, None, :], score_acc, NEG_FILL)
    score_new = jnp.where(allowed[None, None], score_new, NEG_FILL)
    row_max = jnp.maximum(
        jnp.maximum(
            jnp.max(score_old, axis=-1, keepdims=True), jnp.max(score_acc, axis=-1, keepdims=True)
        ),
        jnp.max(score_new, axis=-1, keepdims=True),
    )
    expo_old = jnp.exp(score_old - row_max)
    expo_acc = jnp.exp(score_acc - row_max)
    expo_new = jnp.exp(score_new - row_max)
    denom_sum = (
        jnp.sum(expo_old, axis=-1, keepdims=True)
        + jnp.sum(expo_acc, axis=-1, keepdims=True)
        + jnp.sum(expo_new, axis=-1, keepdims=True)
    )
    probs_old = (expo_old / denom_sum).astype(jnp.bfloat16)
    probs_acc = (expo_acc / denom_sum).astype(jnp.bfloat16)
    probs_new = (expo_new / denom_sum).astype(jnp.bfloat16)
    result = jnp.einsum("kgnm,mkd->nkgd", probs_old, value_old, preferred_element_type=jnp.float32)
    result = result + jnp.einsum(
        "kgnm,mkd->nkgd", probs_acc, value_acc, preferred_element_type=jnp.float32
    )
    result = result + jnp.einsum(
        "kgnm,mkd->nkgd", probs_new, value_new, preferred_element_type=jnp.float32
    )
    return result.reshape(count_new, q_heads * head_dim).astype(jnp.bfloat16)


def route_rows(expert_ids, gate_probs, expert_names, count_rows):
    hit_mask = expert_ids[None, :, :] == expert_names[:, None, None]
    weights = jnp.sum(jnp.where(hit_mask, gate_probs[None], 0.0), axis=2)
    named_int = jnp.any(hit_mask, axis=2).astype(jnp.int32)
    chosen = jnp.argsort(1 - named_int, axis=1, stable=True)[:, :count_rows]
    return (chosen, jnp.take_along_axis(weights, chosen, axis=1))


def body(
    residual_in,
    attn_gain,
    w_query,
    w_keyval,
    query_gain,
    key_gain,
    w_out,
    ffn_gain,
    w_gate,
    w_up,
    w_down,
    key_cache,
    value_cache,
    prefix_lens,
    accepted,
    accept_path,
    parents,
    slot_kinds,
    expert_ids,
    gate_probs,
):
    devices = lax.axis_size("tensor")
    own_index = lax.axis_index("tensor")
    rows_here = residual_in.shape[0]
    model_width = residual_in.shape[1]
    slots_here = key_cache.shape[0]
    count_new = rows_here // slots_here
    row_start = own_index * rows_here
    normed_own = rms_rows(residual_in.astype(jnp.float32), attn_gain).astype(jnp.bfloat16)
    gathered = lax.all_gather(normed_own, "tensor", axis=0, tiled=True)
    query_part = jnp.dot(gathered, w_query, preferred_element_type=jnp.float32).astype(jnp.bfloat16)
    keyval_part = lax.dot_general(
        gathered, w_keyval, (((1,), (1,)), ((), ())), preferred_element_type=jnp.float32
    ).astype(jnp.bfloat16)
    query_tok, keyval_tok = (
        lax.all_to_all(query_part, "tensor", split_axis=0, concat_axis=1, tiled=True),
        lax.all_to_all(keyval_part, "tensor", split_axis=0, concat_axis=1, tiled=True),
    )

    def slot_attend(packed):
        return attend_parts(*packed, query_gain, key_gain)

    attn_own = lax.map(
        slot_attend,
        (
            query_tok.reshape(slots_here, count_new, -1),
            keyval_tok.reshape(slots_here, count_new, -1),
            key_cache,
            value_cache,
            prefix_lens,
            accepted,
            accept_path,
            parents,
            slot_kinds,
        ),
    )
    attn_own = attn_own.reshape(rows_here, -1)
    attn_heads = lax.all_to_all(attn_own, "tensor", split_axis=1, concat_axis=0, tiled=True)
    out_own = lax.psum_scatter(
        jnp.dot(attn_heads, w_out, preferred_element_type=jnp.float32).astype(jnp.bfloat16),
        "tensor",
        scatter_dimension=0,
        tiled=True,
    ).astype(jnp.float32)
    hidden_mid = residual_in.astype(jnp.float32) + out_own
    normed_ffn = rms_rows(hidden_mid, ffn_gain).astype(jnp.bfloat16)
    per_device = w_gate.shape[0]
    top_count = expert_ids.shape[1]
    all_names = jnp.arange(per_device * devices, dtype=jnp.int32)
    own_ids = lax.dynamic_slice_in_dim(expert_ids, row_start, rows_here, 0)
    own_gates = lax.dynamic_slice_in_dim(gate_probs, row_start, rows_here, 0)
    chosen, selected = route_rows(own_ids, own_gates, all_names, rows_here * top_count // EXPERTS)
    send_rows = normed_ffn[chosen]
    received = lax.all_to_all(send_rows, "tensor", split_axis=0, concat_axis=0, tiled=True)
    item_count = received.shape[1]
    grouped = received.reshape(devices, per_device, item_count, model_width)
    gate_val = jnp.einsum("spcd,pfd->spcf", grouped, w_gate, preferred_element_type=jnp.float32)
    up_val = jnp.einsum("spcd,pfd->spcf", grouped, w_up, preferred_element_type=jnp.float32)
    inner_act = (jax.nn.silu(gate_val) * up_val).astype(jnp.bfloat16)
    result = jnp.einsum("spcf,pfd->spcd", inner_act, w_down, preferred_element_type=jnp.float32)
    result = result.reshape(devices * per_device, item_count, model_width)
    returned = lax.all_to_all(
        result.astype(jnp.bfloat16), "tensor", split_axis=0, concat_axis=0, tiled=True
    ).astype(result.dtype)
    scaled = returned * selected[..., None]
    moe_own = (
        jnp.zeros((rows_here, model_width), jnp.float32)
        .at[chosen.reshape(-1)]
        .add(scaled.reshape(-1, model_width))
    )
    return (hidden_mid + moe_own).astype(jnp.bfloat16)


def solution(mesh):
    in_specs = (
        P(("group", "tensor"), None),
        P(),
        P(None, "tensor"),
        P("tensor", None),
        P(),
        P(),
        P("tensor", None),
        P(),
        P("tensor", None, None),
        P("tensor", None, None),
        P("tensor", None, None),
        P(("group", "tensor"), None, None),
        P(("group", "tensor"), None, None),
        P(("group", "tensor")),
        P(("group", "tensor")),
        P(("group", "tensor"), None),
        P(("group", "tensor"), None),
        P(("group", "tensor")),
        P("group", None),
        P("group", None),
    )
    out_specs = P(("group", "tensor"), None)
    return jax.shard_map(body, mesh=mesh, in_specs=in_specs, out_specs=out_specs, check_vma=False)
```

profile of v0, /device:TPU:0, one launch (start us, length us, event | category | flops | bytes accessed | tf_op | source)
XLA Modules:
  0.0 174.6 jit_solution(9839638048949030221)
XLA Ops:
  6.5 1.2 fusion.41
  7.7 1.7 fusion.43
  13.8 2.2 %reshape.279 = bf16[1024,4,128]{2,1,0:T(4,128)(2,1)} reshape(bf16[1,1024,512]{2,1,0:T(8,128)(2,1)} %param.33) | data formatting | bytes 2097152 | tf_op jit(solution)/shard_map/while/body/eval_jaxpr/reshape | solution.py:95
  15.9 2.1 %reshape.283 = bf16[1024,4,128]{2,1,0:T(4,128)(2,1)} reshape(bf16[1,1024,512]{2,1,0:T(8,128)(2,1)} %param.34) | data formatting | bytes 2097152 | tf_op jit(solution)/shard_map/while/body/eval_jaxpr/reshape | solution.py:96
  18.7 2.5 %gather_fusion.2 = bf16[8,512]{1,0:T(8,128)(2,1)} fusion(bf16[1024,512]{1,0:T(8,128)(2,1)} %bitcast.168, s32[1024]{0:T(1024)S(1)} %pad_clamp_fusion.1), kind=kCustom, calls=%fused_computation.clone | custom fusion | bytes 16416 | tf_op jit(solution)/shard_map/while/body/eval_jaxpr/jit(_take)/gather | solution.py:93
  21.2 2.5 %gather_fusion.3 = bf16[8,512]{1,0:T(8,128)(2,1)} fusion(bf16[1024,512]{1,0:T(8,128)(2,1)} %bitcast.169, s32[1024]{0:T(1024)S(1)} %pad_clamp_fusion.1), kind=kCustom, calls=%fused_computation.1.clone | custom fusion | bytes 16416 | tf_op jit(solution)/shard_map/while/body/eval_jaxpr/jit(_take)/gather | solution.py:94
  25.1 10.7 %all-gather.2.cloned.1.call-done = bf16[256,2048]{1,0:T(8,128)(2,1)} async-done(((bf16[32,2048]{1,0:T(8,128)(2,1)}), bf16[256,2048]{1,0:T(8,128)(2,1)}) %all-gather.2.cloned.1.call-update) | async-done | bytes 1048592 | tf_op jit(solution)/shard_map/all_gather | solution.py:184
  35.8 2.4 %convolution_convert_fusion.2 = bf16[256,128]{1,0:T(8,128)(2,1)} fusion(bf16[256,2048]{1,0:T(8,128)(2,1)} %all-gather.2.cloned.1.call-done, bf16[128,2048]{1,0:T(8,128)(2,1)} %param.25), kind=kOutput, calls=%fused_computation.33 | convolution fusion | flops 134250496 | bytes 1638400 | tf_op jit(solution)/shard_map/dot_general | solution.py:186
  38.2 3.4 %all-to-all-start.1 = ((bf16[8,32,128]{2,1,0:T(8,128)(2,1)}), bf16[8,32,128]{2,1,0:T(8,128)(2,1)S(1)}, u32[]{:S(2)}, u32[]{:S(2)}) async-start(bf16[8,32,128]{2,1,0:T(8,128)(2,1)} %bitcast.16), calls=%async_computation.1 | async-start | bytes 131072 | tf_op jit(solution)/shard_map/all_to_all | solution.py:191
  41.6 3.4 %convolution_convert_fusion.1 = bf16[256,512]{1,0:T(8,128)(2,1)} fusion(bf16[256,2048]{1,0:T(8,128)(2,1)} %all-gather.2.cloned.1.call-done, bf16[2048,512]{1,0:T(8,128)(2,1)} %param.24), kind=kOutput, calls=%fused_computation.29 | convolution fusion | flops 537001984 | bytes 3407872 | tf_op jit(solution)/shard_map/dot_general | solution.py:185
  44.9 1.6 all-to-all-done.1
  46.5 3.4 %all-to-all-start = ((bf16[8,32,512]{2,1,0:T(8,128)(2,1)}), bf16[8,32,512]{2,1,0:T(8,128)(2,1)S(1)}, u32[]{:S(2)}, u32[]{:S(2)}) async-start(bf16[8,32,512]{2,1,0:T(8,128)(2,1)} %bitcast.172), calls=%async_computation | async-start | bytes 524288 | tf_op jit(solution)/shard_map/all_to_all | solution.py:190
  53.8 1.4 reshape.285
  55.2 1.4 subtract_convert_fusion.1
  58.0 1.9 %reshape.292 = f32[32,32,128]{2,1,0:T(8,128)} reshape(f32[32,8,512]{2,1,0:T(8,128)} %copy.162) | data formatting | bytes 1048576 | tf_op jit(solution)/shard_map/while/body/eval_jaxpr/convert_element_type | solution.py:80
  59.9 1.3 multiply_reduce_fusion
  61.2 1.2 multiply_multiply_fusion
  62.9 3.4 %bitcast_reduce_fusion = (f32[4,8,32]{1,2,0:T(8,128)S(1)}, f32[4,32,8,1024]{3,2,1,0:T(8,128)}) fusion(pred[1024]{0:T(1024)(128)(4,1)} %fusion.77, bf16[1024,4,128,1]{2,1,0,3:T(4,128)(2,1)S(1)} %bitcast.167, bf16[32,4,8,128]{3,2,1,0:T(8,128)(2,1)S(1)} %pad_maximum_fusion), kind=kOutput, calls=%fused_computation.6 | convolution fusion | flops 271580160 | bytes 5510144 | tf_op jit(solution)/shard_map/while/body/eval_jaxpr/nkgd,mkd->kgnm/dot_general | solution.py:105
  67.0 1.4 fusion.89
  70.4 3.2 %fusion.1 = f32[4,8,32]{1,2,0:T(8,128)S(1)} fusion(f32[4,32,8,1024]{3,2,1,0:T(8,128)} %get-tuple-element.67, f32[4,8,32]{1,2,0:T(8,128)S(1)} %copy.174, pred[1024]{0:T(1024)(128)(4,1)} %fusion.77), kind=kLoop, calls=%fused_computation.10 | loop fusion | flops 4193280 | bytes 4203520 | tf_op jit(solution)/shard_map/while/body/eval_jaxpr/reduce_sum | solution.py:129
  79.5 3.7 %fusion.12 = f32[32,4,8,128]{3,2,0,1:T(8,128)S(1)} fusion(f32[4,32,8,1024]{3,2,1,0:T(8,128)} %get-tuple-element.67, f32[4,8,32]{1,2,0:T(8,128)S(1)} %copy.176, f32[4,8,32]{1,2,0:T(8,128)} %copy-done.4, pred[1024]{0:T(1024)(128)(4,1)} %fusion.77, bf16[1024,4,128,1]{2,1,0,3:T(4,128)(2,1)} %bitcast.170), kind=kOutput, calls=%fused_computation.20 | convolution fusion | flops 273678336 | bytes 5776384 | tf_op jit(solution)/shard_map/while/body/eval_jaxpr/kgnm,mkd->nkgd/dot_general | solution.py:136
  85.7 10.6 %all_to_all.55 = bf16[32,8,512]{2,0,1:T(8,128)(2,1)S(1)} all-to-all(bf16[32,8,512]{2,0,1:T(8,128)(2,1)S(1)} %copy.182), channel_id=1, replica_groups=mesh['group'=4,'tensor'=8] {'tensor'}, dimensions={1} | all-to-all | bytes 524288 | tf_op jit(solution)/shard_map/all_to_all | solution.py:212
  96.3 3.3 %convolution_convert_fusion = bf16[256,2048]{1,0:T(8,128)(2,1)} fusion(bf16[256,512]{1,0:T(8,128)(2,1)S(1)} %bitcast.171, bf16[512,2048]{1,0:T(8,128)(2,1)} %param.28), kind=kOutput, calls=%fused_computation.17 | convolution fusion | flops 537395200 | bytes 3407872 | tf_op jit(solution)/shard_map/dot_general | solution.py:214
  102.5 32.5 %reduce-scatter.2.cloned.1.call-done = bf16[32,2048]{1,0:T(8,128)(2,1)} async-done(((bf16[256,2048]{1,0:T(8,128)(2,1)}), bf16[32,2048]{1,0:T(8,128)(2,1)}) %reduce-scatter.2.cloned.1.call-update) | async-done | bytes 131088 | tf_op jit(solution)/shard_map/reduce_scatter | solution.py:213
  137.1 1.2 gather_fusion
  138.3 1.5 reshape.312
  139.8 3.5 %all-to-all-start.3 = ((bf16[8,2,2048]{2,1,0:T(2,128)(2,1)}), bf16[8,2,2048]{2,1,0:T(2,128)(2,1)S(1)}, u32[]{:S(2)}, u32[]{:S(2)}) async-start(bf16[8,2,2048]{2,1,0:T(2,128)(2,1)} %reshape.312), calls=%async_computation.4 | async-start | bytes 131072 | tf_op jit(solution)/shard_map/all_to_all | solution.py:228
  144.2 3.9 %all-to-all-done.3 = bf16[8,2,2048]{2,1,0:T(2,128)(2,1)S(1)} async-done(((bf16[8,2,2048]{2,1,0:T(2,128)(2,1)}), bf16[8,2,2048]{2,1,0:T(2,128)(2,1)S(1)}, u32[]{:S(2)}, u32[]{:S(2)}) %all-to-all-start.3) | async-done | bytes 65568 | tf_op jit(solution)/shard_map/all_to_all | solution.py:228
  148.1 3.4 %fusion.20 = f32[8,1,2,768]{3,0,2,1:T(8,128)} fusion(bf16[1,768,2048]{2,1,0:T(8,128)(2,1)} %param.30, bf16[8,2,2048]{2,1,0:T(2,128)(2,1)S(1)} %all-to-all-done.3), kind=kOutput, calls=%fused_computation.34 | convolution fusion | flops 50331648 | bytes 3260416 | tf_op jit(solution)/shard_map/spcd,pfd->spcf/dot_general | solution.py:231
  151.6 3.8 %fusion.8 = bf16[8,2,2048]{2,0,1:T(8,128)(2,1)S(1)} fusion(bf16[1,768,2048]{2,1,0:T(8,128)(2,1)S(1)} %copy-done, bf16[1,768,2048]{2,1,0:T(8,128)(2,1)} %param.31, bf16[8,2,2048]{2,1,0:T(2,128)(2,1)S(1)} %all-to-all-done.3, f32[8,1,2,768]{3,0,2,1:T(8,128)} %fusion.20), kind=kOutput, calls=%fused_computation.18 | convolution fusion | flops 100769792 | bytes 6471680 | tf_op jit(solution)/shard_map/spcf,pfd->spcd/dot_general | solution.py:234
  156.1 3.4 %all-to-all-start.4 = ((bf16[8,2,2048]{2,1,0:T(2,128)(2,1)}), bf16[8,2,2048]{2,1,0:T(2,128)(2,1)S(1)}, u32[]{:S(2)}, u32[]{:S(2)}) async-start(bf16[8,2,2048]{2,1,0:T(2,128)(2,1)} %copy.188), calls=%async_computation.5 | async-start | bytes 131072 | tf_op jit(solution)/shard_map/all_to_all | solution.py:236
  159.5 4.9 %all-to-all-done.4 = bf16[8,2,2048]{2,1,0:T(2,128)(2,1)S(1)} async-done(((bf16[8,2,2048]{2,1,0:T(2,128)(2,1)}), bf16[8,2,2048]{2,1,0:T(2,128)(2,1)S(1)}, u32[]{:S(2)}, u32[]{:S(2)}) %all-to-all-start.4) | async-done | bytes 65568 | tf_op jit(solution)/shard_map/all_to_all | solution.py:236
  (114 shorter events, 30.8 us)
Async XLA Ops:
  6.5 145.0 %copy-start = (bf16[1,768,2048]{2,1,0:T(8,128)(2,1)S(1)}, bf16[1,768,2048]{2,1,0:T(8,128)(2,1)}, u32[]{:S(2)}) copy-start(bf16[1,768,2048]{2,1,0:T(8,128)(2,1)} %param.32) | copy-start | bytes 9437188
  6.5 11.5 %copy-start.16 = (s32[1,8]{1,0:T(1,128)S(1)}, s32[1,8]{1,0:T(1,128)}, u32[]{:S(2)}) copy-start(s32[1,8]{1,0:T(1,128)} %param.37) | copy-start | bytes 100
  6.5 29.2 %all-gather.2.cloned.1.call-start = ((), (), s32[]{:S(2)}) async-start(), calls=%async_computation.6 | async-start | bytes 1179648 | tf_op jit(solution)/shard_map/all_gather | solution.py:184
  38.2 8.3 %all-to-all-start.1 = ((bf16[8,32,128]{2,1,0:T(8,128)(2,1)}), bf16[8,32,128]{2,1,0:T(8,128)(2,1)S(1)}, u32[]{:S(2)}, u32[]{:S(2)}) async-start(bf16[8,32,128]{2,1,0:T(8,128)(2,1)} %bitcast.16), calls=%async_computation.1 | async-start | bytes 131072 | tf_op jit(solution)/shard_map/all_to_all | solution.py:191
  46.5 10.3 %all-to-all-start = ((bf16[8,32,512]{2,1,0:T(8,128)(2,1)}), bf16[8,32,512]{2,1,0:T(8,128)(2,1)S(1)}, u32[]{:S(2)}, u32[]{:S(2)}) async-start(bf16[8,32,512]{2,1,0:T(8,128)(2,1)} %bitcast.172), calls=%async_computation | async-start | bytes 524288 | tf_op jit(solution)/shard_map/all_to_all | solution.py:190
  49.9 85.0 %reduce-scatter.2.cloned.1.call-start = ((), (), s32[]{:S(2)}) async-start(), calls=%async_computation.7 | async-start | bytes 1179648 | tf_op jit(solution)/shard_map/reduce_scatter | solution.py:213
  53.8 8.7 %copy-start.6 = (f32[32,64]{1,0:T(8,128)S(1)}, f32[32,64]{1,0:T(8,128)}, u32[]{:S(2)}) copy-start(f32[32,64]{1,0:T(8,128)} %get-tuple-element.61) | copy-start | bytes 24580
  59.9 3.0 %copy-start.1 = (bf16[1024,4,128]{2,1,0:T(4,128)(2,1)S(1)}, bf16[1024,4,128]{2,1,0:T(4,128)(2,1)}, u32[]{:S(2)}) copy-start(bf16[1024,4,128]{2,1,0:T(4,128)(2,1)} %reshape.279) | copy-start | bytes 3145732
  62.7 4.2 %copy-start.8 = (bf16[32,4,64]{2,0,1:T(8,128)(2,1)S(1)}, bf16[32,4,64]{2,0,1:T(8,128)(2,1)}, u32[]{:S(2)}) copy-start(bf16[32,4,64]{2,0,1:T(8,128)(2,1)} %get-tuple-element.52) | copy-start | bytes 49156
  62.7 4.2 %copy-start.10 = (pred[32,32]{0,1:T(8,128)(4,1)S(1)}, pred[32,32]{0,1:T(8,128)(4,1)}, u32[]{:S(2)}) copy-start(pred[32,32]{0,1:T(8,128)(4,1)} %copy.169) | copy-start | bytes 3076
  70.3 4.5 %copy-start.4 = (f32[4,8,32]{1,2,0:T(8,128)}, f32[4,8,32]{1,2,0:T(8,128)S(1)}, u32[]{:S(2)}) copy-start(f32[4,8,32]{1,2,0:T(8,128)S(1)} %copy.174) | copy-start | bytes 12292
  74.9 1.2 copy-start.5
  79.4 3.7 %copy-start.9 = (bf16[8,512]{1,0:T(8,128)(2,1)S(1)}, bf16[8,512]{1,0:T(8,128)(2,1)}, u32[]{:S(2)}) copy-start(bf16[8,512]{1,0:T(8,128)(2,1)} %gather_fusion.3) | copy-start | bytes 24580
  79.5 3.7 %copy-start.12 = (pred[8]{0:T(512)(128)(4,1)S(1)}, pred[8]{0:T(512)(128)(4,1)}, u32[]{:S(2)}) copy-start(pred[8]{0:T(512)(128)(4,1)} %get-tuple-element.32) | copy-start | bytes 28
  79.5 4.0 %copy-start.3 = (bf16[4,8,32,32]{3,1,2,0:T(8,128)(2,1)S(1)}, bf16[4,8,32,32]{3,1,2,0:T(8,128)(2,1)}, u32[]{:S(2)}) copy-start(bf16[4,8,32,32]{3,1,2,0:T(8,128)(2,1)} %copy.180) | copy-start | bytes 196612
  79.5 4.0 %copy-start.7 = (bf16[32,4,128]{2,1,0:T(4,128)(2,1)S(1)}, bf16[32,4,128]{2,1,0:T(4,128)(2,1)}, u32[]{:S(2)}) copy-start(bf16[32,4,128]{2,1,0:T(4,128)(2,1)} %reshape.285) | copy-start | bytes 98308
  83.2 16.4 %copy-start.13 = (s32[256,8]{0,1:T(8,128)S(1)}, s32[256,8]{0,1:T(8,128)}, u32[]{:S(2)}) copy-start(s32[256,8]{0,1:T(8,128)} %param.40) | copy-start | bytes 24580
  83.5 17.5 %copy-start.14 = (f32[256,8]{0,1:T(8,128)S(1)}, f32[256,8]{0,1:T(8,128)}, u32[]{:S(2)}) copy-start(f32[256,8]{0,1:T(8,128)} %param.41) | copy-start | bytes 24580
  96.3 38.7 %copy-start.2 = (bf16[32,2048]{1,0:T(8,128)(2,1)S(1)}, bf16[32,2048]{1,0:T(8,128)(2,1)}, u32[]{:S(2)}) copy-start(bf16[32,2048]{1,0:T(8,128)(2,1)} %param.22) | copy-start | bytes 393220
  96.3 39.8 %copy-start.11 = (f32[2048]{0:T(1024)S(1)}, f32[2048]{0:T(1024)}, u32[]{:S(2)}) copy-start(f32[2048]{0:T(1024)} %param.29) | copy-start | bytes 24580
  100.6 35.4 %copy-start.15 = (s32[8,32]{0,1:T(8,128)}, s32[8,32]{0,1:T(8,128)S(1)}, u32[]{:S(2)}) copy-start(s32[8,32]{0,1:T(8,128)S(1)} %get-tuple-element.31) | copy-start | bytes 3076
  139.8 8.3 %all-to-all-start.3 = ((bf16[8,2,2048]{2,1,0:T(2,128)(2,1)}), bf16[8,2,2048]{2,1,0:T(2,128)(2,1)S(1)}, u32[]{:S(2)}, u32[]{:S(2)}) async-start(bf16[8,2,2048]{2,1,0:T(2,128)(2,1)} %reshape.312), calls=%async_computation.4 | async-start | bytes 131072 | tf_op jit(solution)/shard_map/all_to_all | solution.py:228
  156.1 8.3 %all-to-all-start.4 = ((bf16[8,2,2048]{2,1,0:T(2,128)(2,1)}), bf16[8,2,2048]{2,1,0:T(2,128)(2,1)S(1)}, u32[]{:S(2)}, u32[]{:S(2)}) async-start(bf16[8,2,2048]{2,1,0:T(2,128)(2,1)} %copy.188), calls=%async_computation.5 | async-start | bytes 131072 | tf_op jit(solution)/shard_map/all_to_all | solution.py:236
Sparse Core Ops, SparseCore 0:
  9.6 26.1 all-gather.1
  99.7 35.1 reduce-scatter.1
where the time goes:
time: 176 us; the launch traced here: 175 us
  waiting for transfers between devices  53.8 us (31%)
  local copies, waits for them, and re-layouts  28.3 us (16%)
  matrix products  28.1 us (16%)
  other arithmetic  24.4 us (14%)
  between operations  15.8 us (9%)
  starting transfers between devices  13.7 us (8%)
  blocking collectives  10.6 us (6%)
    reduce_scatter x1, waiting for transfers between devices, body(): lax.psum_scatter(jnp.dot(attn_heads, w_out, preferred_element_type=jnp.fl...  32.5 us
    all_gather x1, waiting for transfers between devices, body(): gathered = lax.all_gather(normed_own, 'tensor', axis=0, tiled=True)  10.7 us
    all_to_all x1, blocking collectives, body(): lax.all_to_all(attn_own, 'tensor', split_axis=1, concat_axis=0, tiled=True)  10.6 us
    all_to_all x1, waiting for transfers between devices, body(): lax.all_to_all(result.astype(jnp.bfloat16), 'tensor', split_axis=0, conca...  4.86 us
    reduce_sum x4, other arithmetic, rms_rows(): jnp.mean(values * values, axis=-1, keepdims=True) + EPSILON  4.31 us
    all_to_all x1, waiting for transfers between devices, body(): lax.all_to_all(send_rows, 'tensor', split_axis=0, concat_axis=0, tiled=True)  3.92 us
    dot_general x1, matrix products, body(): jnp.einsum('spcf,pfd->spcd', inner_act, w_down, preferred_element_type=jn...  3.79 us
    dot_general x1, matrix products, attend_parts(): jnp.einsum('kgnm,mkd->nkgd', probs_old, value_old, preferred_element_type...  3.68 us
  transfers between devices with their start and end apart: 6, of which 6 were waited for; matrix products, arithmetic and copies ran while one was open for 16% of the time, Pallas kernels for 0%

commit v1 on v0

v1 whole, which is shorter than its diff:
```python
import functools
import math

import jax
import jax.numpy as jnp
import numpy as np
from jax import lax
from jax.experimental import pallas as pl
from jax.experimental.pallas import tpu as pltpu
from jax.sharding import PartitionSpec as P

EXPERTS = 128
SINK = 4
WIN = 512

EPSILON = 1e-06
NEG_FILL = -1e30
ROPE_BASE = 1000000.0
LOG2E = math.log2(math.e)
F32 = jnp.float32
BF16 = jnp.bfloat16
MIB = 1 << 20


def iota(shape, dim):
    return lax.broadcasted_iota(jnp.int32, shape, dim)


def dot_last(left, right):
    return lax.dot_general(left, right, (((1,), (1,)), ((), ())), preferred_element_type=F32)


def norm_rows(values):
    return values * lax.rsqrt(jnp.mean(values * values, axis=-1, keepdims=True) + EPSILON)


def call(kernel, name, outs, args, scratch=(), limit=16, flops=0, moved=0):
    many = isinstance(outs, (list, tuple))
    specs = [pl.BlockSpec(memory_space=pltpu.VMEM) for _ in (outs if many else [outs])]
    return pl.pallas_call(
        kernel,
        out_shape=outs,
        in_specs=[pl.BlockSpec(memory_space=space) for _, space in args],
        out_specs=specs if many else specs[0],
        scratch_shapes=list(scratch),
        compiler_params=pltpu.CompilerParams(vmem_limit_bytes=limit * MIB),
        cost_estimate=pl.CostEstimate(flops=flops, bytes_accessed=moved, transcendentals=0),
        name=name,
    )(*[array for array, _ in args])


def exchange(blocks):
    return lax.all_to_all(blocks, "tensor", split_axis=0, concat_axis=0, tiled=True)


def gather_blocks(block, devices):
    def hop(value, step):
        return lax.ppermute(value, "tensor", [(i, i ^ step) for i in range(devices)])

    got = {0: block}
    for step in range(2, devices, 2):
        got[step] = hop(block, step)
    got[1] = hop(block, 1)
    for step in range(2, devices, 2):
        got[step + 1] = hop(got[step], 1)
    return [got[step] for step in range(devices)]


def window_rows(path_len):
    return -(-(WIN + 2 * (path_len - 1) + 16) // 16) * 16


def prep_kernel(
    per,
    key_cache,
    value_cache,
    prefix_ref,
    accepted_ref,
    path_ref,
    kind_ref,
    parents_ref,
    ids_ref,
    gates_ref,
    freq_ref,
    keys_ref,
    values_ref,
    mask_ref,
    cos_ref,
    sin_ref,
    pick_ref,
    combine_ref,
    weight_ref,
    hit_ref,
    rank_ref,
    own_ref,
    sems,
):
    me = lax.axis_index("tensor")
    new = parents_ref.shape[1]
    cache_len = key_cache.shape[1]
    path_len = path_ref.shape[1]
    wide = window_rows(path_len)
    sink_at, win_at = new, new + 16
    end = win_at + wide
    prefix = prefix_ref[0]
    accepted = accepted_ref[0]
    total = prefix + accepted
    low = jnp.maximum(total - WIN, 0)
    start = pl.multiple_of(jnp.minimum((low // 16) * 16, cache_len - wide), 16)
    copies = []
    for which, (cache, buf) in enumerate(((key_cache, keys_ref), (value_cache, values_ref))):
        copies.append(
            pltpu.make_async_copy(
                cache.at[0, pl.ds(start, wide)], buf.at[pl.ds(win_at, wide)], sems.at[which, 0]
            )
        )
        copies.append(
            pltpu.make_async_copy(
                cache.at[0, pl.ds(0, 16)], buf.at[pl.ds(sink_at, 16)], sems.at[which, 1]
            )
        )
    for copy in copies:
        copy.start()

    span, width = keys_ref.shape
    for buf in (keys_ref, values_ref):
        buf[0:new, :] = jnp.zeros((new, width), BF16)
        buf[end:span, :] = jnp.zeros((span - end, width), BF16)

    column = iota((1, span), 1)
    row = jnp.where(column < win_at, column - sink_at, start + column - win_at)
    taken = jnp.zeros((1, span), jnp.bool_)
    for step in range(path_len):
        taken = taken | ((row == prefix + path_ref[0, step]) & (step < accepted))
    old = (row < prefix) & ((row < SINK) | (row >= total - WIN))
    in_window = (column >= win_at) & (column < end) & (old | taken)
    in_sink = (column >= sink_at) & (column < win_at) & (row < SINK) & (row < prefix) & (start > 0)
    seen = jnp.where(in_window | in_sink, 0.0, NEG_FILL)
    mask_ref[...] = jnp.broadcast_to(seen, mask_ref.shape)

    down, across = iota((new, new), 0), iota((new, new), 1)
    eye = (down == across).astype(F32)
    back = eye + (down == parents_ref[...]).astype(F32)
    for _ in range((new - 1).bit_length()):
        half = back.astype(BF16)
        back = jnp.minimum(jnp.dot(half, half, preferred_element_type=F32), 1.0)
    reach = lax.dot_general(
        back.astype(BF16), eye.astype(BF16), (((0,), (0,)), ((), ())), preferred_element_type=F32
    )
    tree = (kind_ref[0] == 1).astype(F32)
    causal = (across <= down).astype(F32)
    allowed = tree * reach + (1.0 - tree) * causal
    mask_ref[:, 0:new] = jnp.where(allowed > 0.5, 0.0, NEG_FILL)
    depth = tree * (jnp.sum(reach, axis=1, keepdims=True) - 1.0)
    depth = depth + (1.0 - tree) * iota((new, 1), 0).astype(F32)
    angle = (total.astype(F32) + depth) * freq_ref[...]
    lane = iota(angle.shape, 1)
    sine = jnp.sin(angle)
    cos_ref[...] = jnp.cos(angle)
    sin_ref[...] = jnp.where(lane < angle.shape[1] // 2, -sine, sine)

    tokens = ids_ref.shape[1]
    slots = tokens // new
    experts = hit_ref.shape[0]
    ids = ids_ref[...]
    for expert in range(experts):
        hit_ref[expert : expert + 1, :] = jnp.max(
            (ids == expert).astype(F32), axis=0, keepdims=True
        )
    before, after = iota((tokens, tokens), 0), iota((tokens, tokens), 1)
    earlier = (before < after) & (before // new == after // new)
    rank_ref[...] = jnp.dot(
        hit_ref[...].astype(BF16), earlier.astype(BF16), preferred_element_type=F32
    )
    rows = slots * per
    slot_of = iota((rows, tokens), 1) // new
    row_slot = iota((rows, tokens), 0) // per
    row_rank = (iota((rows, tokens), 0) % per).astype(F32)
    same = slot_of == row_slot
    mine = iota((1, tokens), 1) // new == me
    for expert in range(experts):
        hit = hit_ref[expert : expert + 1, :]
        rank = rank_ref[expert : expert + 1, :]
        chosen = same & (hit > 0.5) & (rank == row_rank)
        pick_ref[expert * rows : (expert + 1) * rows, :] = chosen.astype(F32).astype(BF16)
        for place in range(per):
            at = expert * per + place
            own = mine & (hit > 0.5) & (rank == float(place))
            own_ref[at : at + 1, :] = own.astype(F32)
    shift = iota((tokens, new), 0) == me * new + iota((tokens, new), 1)
    combine_ref[...] = lax.dot_general(
        shift.astype(F32).astype(BF16),
        own_ref[...].astype(BF16),
        (((0,), (1,)), ((), ())),
        preferred_element_type=F32,
    )
    weight = jnp.sum(jnp.where(ids == me, gates_ref[...], 0.0), axis=0, keepdims=True)
    hit = jnp.max((ids == me).astype(F32), axis=0, keepdims=True)
    rank = rank_ref[pl.ds(me, 1), :]
    chosen = same & (hit > 0.5) & (rank == row_rank)
    chosen_weight = jnp.sum(jnp.where(chosen, weight, 0.0), axis=1, keepdims=True)
    weight_ref[...] = jnp.broadcast_to(chosen_weight, weight_ref.shape)
    for copy in copies:
        copy.wait()


def project_kernel(devices, *refs):
    blocks = refs[:devices]
    gain_ref, wq_ref, wkv_ref, out_ref, raw_ref, normed = refs[devices:]
    me = lax.axis_index("tensor")
    rows = blocks[0].shape[0]
    gain = gain_ref[...]
    for step in range(devices):
        at = pl.multiple_of((me ^ step) * rows, rows)
        block = blocks[step][...]
        raw_ref[pl.ds(at, rows), :] = block
        normed[pl.ds(at, rows), :] = (norm_rows(block.astype(F32)) * gain).astype(BF16)
    wide = wq_ref.shape[1]
    values = normed[...]
    query = jnp.dot(values, wq_ref[...], preferred_element_type=F32).astype(BF16)
    keyval = dot_last(values, wkv_ref[...]).astype(BF16)
    out_ref[:, :, :wide] = query.reshape(devices, rows, wide)
    out_ref[:, :, wide:] = keyval.reshape(devices, rows, -1)


def attend_kernel(
    q_width,
    head,
    got_ref,
    *refs,
):
    (
        q_gain_ref,
        k_gain_ref,
        keys_in,
        values_in,
        mask_ref,
        cos_ref,
        sin_ref,
        out_ref,
        keys_ref,
        values_ref,
    ) = refs[-10:]
    devices, new, _ = got_ref.shape
    span, kv_width = keys_in.shape
    kv_heads = kv_width // head
    per_device = q_width // head
    group = devices * per_device // kv_heads
    cos, sin = cos_ref[...], sin_ref[...]

    def rope(values):
        return values * cos + pltpu.roll(values, head // 2, 1) * sin

    def fresh(piece):
        if len(refs) > 10:
            return refs[0][:, piece * head : (piece + 1) * head]
        return got_ref[piece, :, q_width : q_width + head]

    keys_ref[...] = keys_in[...]
    values_ref[...] = values_in[...]
    scale = head ** (-0.5) * LOG2E
    for kv in range(kv_heads):
        cols = slice(kv * head, (kv + 1) * head)
        key_new = rope(norm_rows(fresh(kv).astype(F32)) * k_gain_ref[...])
        keys_ref[0:new, cols] = key_new.astype(BF16)
        values_ref[0:new, cols] = fresh(kv_heads + kv)
        queries = []
        for member in range(group):
            device, part = divmod(kv * group + member, per_device)
            raw = got_ref[device, :, part * head : (part + 1) * head].astype(F32)
            queries.append(rope(norm_rows(raw) * q_gain_ref[...]).astype(BF16))
        query = jnp.concatenate(queries, axis=0)
        score = dot_last(query, keys_ref[:, cols]) * scale
        score = score.reshape(group, new, span) + mask_ref[...][None]
        expo = jnp.exp2(score - jnp.max(score, axis=-1, keepdims=True))
        denom = jnp.sum(expo, axis=-1, keepdims=True).reshape(group * new, 1)
        expo = expo.astype(BF16).reshape(group * new, span)
        result = jnp.dot(expo, values_ref[:, cols], preferred_element_type=F32) / denom
        result = result.astype(BF16)
        for member in range(group):
            device, part = divmod(kv * group + member, per_device)
            out_ref[device, :, part * head : (part + 1) * head] = result[
                member * new : (member + 1) * new
            ]


def spread_kernel(got_ref, pick_ref, w_ref, out_ref, rows_ref):
    slots, new, depth = got_ref.shape
    extra = rows_ref.shape[1] - new
    heads = got_ref[...].reshape(slots * new, depth)
    picked = jnp.dot(pick_ref[...], heads, preferred_element_type=F32).astype(BF16)
    rows_ref[:, 0:new, :] = got_ref[...]
    rows_ref[:, new:, :] = picked.reshape(slots, extra, depth)
    left = rows_ref[...].reshape(slots * (new + extra), depth)
    width = w_ref.shape[1]
    tile = min(512, width)
    for at in range(0, width, tile):
        part = jnp.dot(left, w_ref[:, at : at + tile], preferred_element_type=F32)
        out_ref[:, :, at : at + tile] = part.astype(BF16).reshape(slots, new + extra, tile)


def select_kernel(pick_ref, raw_ref, out_ref):
    me = lax.axis_index("tensor")
    rows = out_ref.shape[0]
    pick = pick_ref[pl.ds(pl.multiple_of(me * rows, rows), rows), :]
    out_ref[...] = jnp.dot(pick, raw_ref[...], preferred_element_type=F32)


def expert_kernel(
    got_ref, own_ref, picked_ref, gain_ref, weight_ref, wg_ref, wu_ref, wd_ref, out_ref, hidden_ref
):
    devices, rows, width = got_ref.shape
    new = own_ref.shape[0]
    per = out_ref.shape[1]
    total = got_ref[0].astype(F32)
    for source in range(1, devices):
        total = total + got_ref[source].astype(F32)
    hidden_ref[...] = own_ref[...].astype(F32) + total[:new]
    hidden = picked_ref[...] + total[new:]
    normed = (norm_rows(hidden) * gain_ref[...]).astype(BF16)
    gate = dot_last(normed, wg_ref[0])
    up = dot_last(normed, wu_ref[0])
    inner = (gate / (1.0 + jnp.exp(-gate)) * up).astype(BF16)
    result = jnp.dot(inner, wd_ref[0], preferred_element_type=F32) * weight_ref[:, 0:1]
    for slot in range(out_ref.shape[0]):
        out_ref[slot] = result[slot * per : (slot + 1) * per].astype(BF16)


def combine_kernel(hidden_ref, got_ref, combine_ref, out_ref, rows_ref):
    experts, per, width = got_ref.shape
    for expert in range(experts):
        rows_ref[expert * per : (expert + 1) * per, :] = got_ref[expert].astype(F32)
    moe = jnp.dot(
        combine_ref[...].astype(BF16), rows_ref[...].astype(BF16), preferred_element_type=F32
    )
    out_ref[...] = (hidden_ref[...] + moe).astype(BF16)


def body(
    residual_in,
    attn_gain,
    w_query,
    w_keyval,
    query_gain,
    key_gain,
    w_out,
    ffn_gain,
    w_gate,
    w_up,
    w_down,
    key_cache,
    value_cache,
    prefix_lens,
    accepted,
    accept_path,
    parents,
    slot_kinds,
    expert_ids,
    gate_probs,
):
    devices = lax.axis_size("tensor")
    new, width = residual_in.shape
    head = query_gain.shape[0]
    kv_width = key_cache.shape[2]
    q_width = w_query.shape[1]
    new_width = w_keyval.shape[0]
    tokens, top = expert_ids.shape
    per = new * top // EXPERTS
    held = devices * w_gate.shape[0]
    rows = devices * per
    assert key_cache.shape[0] == 1 and w_gate.shape[0] == 1
    vmem, smem, any_space = pltpu.VMEM, pltpu.SMEM, pl.ANY
    shape = jax.ShapeDtypeStruct

    blocks = gather_blocks(residual_in, devices)

    freq = ROPE_BASE ** (-2.0 * np.arange(head // 2) / head)
    freq = jnp.asarray(np.concatenate([freq, freq])[None, :], F32)
    span = -(-(new + 16 + window_rows(accept_path.shape[1])) // 128) * 128
    keys, values, mask, cos, sin, pick, combine, weight = call(
        functools.partial(prep_kernel, per),
        "prep",
        [
            shape((span, kv_width), BF16),
            shape((span, kv_width), BF16),
            shape((new, span), F32),
            shape((new, head), F32),
            shape((new, head), F32),
            shape((held * rows, tokens), BF16),
            shape((new, held * per), F32),
            shape((rows, 128), F32),
        ],
        [
            (key_cache, any_space),
            (value_cache, any_space),
            (prefix_lens, smem),
            (accepted, smem),
            (accept_path, smem),
            (slot_kinds, smem),
            (parents, vmem),
            (expert_ids.T, vmem),
            (gate_probs.T, vmem),
            (freq, vmem),
        ],
        [
            pltpu.VMEM((held, tokens), F32),
            pltpu.VMEM((held, tokens), F32),
            pltpu.VMEM((held * per, tokens), F32),
            pltpu.SemaphoreType.DMA((2, 2)),
        ],
        limit=24,
        moved=4 * span * kv_width * 2,
    )

    projected, raw = call(
        functools.partial(project_kernel, devices),
        "project",
        [
            shape((devices, new, q_width + new_width), BF16),
            shape((tokens, width), BF16),
        ],
        [(block, vmem) for block in blocks]
        + [(attn_gain[None, :], vmem), (w_query, vmem), (w_keyval, vmem)],
        [pltpu.VMEM((tokens, width), BF16)],
        limit=32,
        flops=2 * tokens * width * (q_width + new_width),
        moved=2 * width * (q_width + new_width),
    )
    got = exchange(projected)
    picked_in = call(
        select_kernel,
        "select",
        shape((rows, width), F32),
        [(pick, vmem), (raw, vmem)],
        flops=2 * rows * width * tokens,
        moved=2 * tokens * width,
    )

    extra = []
    if new_width % head:
        extra = [(got[:, :, q_width:].transpose(1, 0, 2).reshape(new, -1), vmem)]
    attended = call(
        functools.partial(attend_kernel, q_width, head),
        "attend",
        shape((devices, new, q_width), BF16),
        [(got, vmem)]
        + extra
        + [
            (query_gain[None, :], vmem),
            (key_gain[None, :], vmem),
            (keys, vmem),
            (values, vmem),
            (mask, vmem),
            (cos, vmem),
            (sin, vmem),
        ],
        [pltpu.VMEM((span, kv_width), BF16), pltpu.VMEM((span, kv_width), BF16)],
        limit=24,
        flops=4 * new * devices * q_width * span,
        moved=4 * span * kv_width,
    )
    heads = exchange(attended)

    partial = call(
        spread_kernel,
        "spread",
        shape((devices, new + rows, width), BF16),
        [(heads, vmem), (pick, vmem), (w_out, vmem)],
        [pltpu.VMEM((devices, new + rows, q_width), BF16)],
        limit=32,
        flops=2 * devices * (new + rows) * width * q_width,
        moved=2 * q_width * width,
    )
    partials = exchange(partial)

    result, hidden = call(
        expert_kernel,
        "expert",
        [shape((devices, per, width), BF16), shape((new, width), F32)],
        [
            (partials, vmem),
            (residual_in, vmem),
            (picked_in, vmem),
            (ffn_gain[None, :], vmem),
            (weight, vmem),
            (w_gate, vmem),
            (w_up, vmem),
            (w_down, vmem),
        ],
        limit=40,
        flops=6 * rows * width * w_gate.shape[1],
        moved=6 * width * w_gate.shape[1],
    )
    returned = exchange(result)
    return call(
        combine_kernel,
        "combine",
        shape((new, width), BF16),
        [(hidden, vmem), (returned, vmem), (combine, vmem)],
        [pltpu.VMEM((held * per, width), F32)],
        moved=6 * new * width,
    )


def solution(mesh):
    in_specs = (
        P(("group", "tensor"), None),
        P(),
        P(None, "tensor"),
        P("tensor", None),
        P(),
        P(),
        P("tensor", None),
        P(),
        P("tensor", None, None),
        P("tensor", None, None),
        P("tensor", None, None),
        P(("group", "tensor"), None, None),
        P(("group", "tensor"), None, None),
        P(("group", "tensor")),
        P(("group", "tensor")),
        P(("group", "tensor"), None),
        P(("group", "tensor"), None),
        P(("group", "tensor")),
        P("group", None),
        P("group", None),
    )
    out_specs = P(("group", "tensor"), None)
    return jax.shard_map(body, mesh=mesh, in_specs=in_specs, out_specs=out_specs, check_vma=False)
```

time: 176 us -> 98.1 us (0.56)
  matrix products: 28.1 us -> 0 us
  waiting for transfers between devices: 53.8 us -> 28 us
  other arithmetic: 24.4 us -> 0 us
  between operations: 15.8 us -> 2.04 us
  Pallas kernels: 0 us -> 12 us
  blocking collectives: 10.6 us -> 18.3 us
  local copies, waits for them, and re-layouts: 28.3 us -> 24.9 us
  starting transfers between devices: 13.7 us -> 11.9 us
    reduce_scatter x1 -> x0, waiting for transfers between devices: 32.5 us -> none  [body(): lax.psum_scatter(jnp.dot(attn_heads, w_out, preferred_element_type=jnp.fl...]
    dot_general x16 -> x0, matrix products: 28.1 us -> none  [the longest x1 3.79 us: body(): jnp.einsum('spcf,pfd->spcd', inner_act, w_down, preferred_element_type=jn...]
    unnamed x34 -> x62, local copies, waits for them, and re-layouts: 0.08 us -> 24.9 us
    pallas_call x0 -> x7, Pallas kernels: none -> 12 us  [call(): pl.pallas_call(kernel, out_shape=outs, in_specs=[pl.BlockSpec(memory_spac...]
    all_gather x1 -> x0, waiting for transfers between devices: 10.7 us -> none  [body(): gathered = lax.all_gather(normed_own, 'tensor', axis=0, tiled=True)]
    all_to_all x4 -> x2, waiting for transfers between devices: 10.6 us -> 20.7 us  [exchange(): lax.all_to_all(blocks, 'tensor', split_axis=0, concat_axis=0, tiled=True)]
    gather x9 -> x0, local copies, waits for them, and re-layouts: 9.35 us -> none  [the longest x2 2.74 us: body(): send_rows = normed_ffn[chosen]]
    reduce_sum x8 -> x0, other arithmetic: 8.74 us -> none  [the longest x4 4.31 us: rms_rows(): jnp.mean(values * values, axis=-1, keepdims=True) + EPSILON]
  transfers between devices with their start and end apart: 6 -> 9, of which waited for: 6 -> 6; matrix products, arithmetic and copies ran while one was open for 16% -> 0% of each run, Pallas kernels for 0% -> 2%
where the time goes in v1:
time: 98.1 us; the launch traced here: 97.1 us
  waiting for transfers between devices  28 us (29%)
  local copies, waits for them, and re-layouts  24.9 us (25%)
  blocking collectives  18.3 us (19%)
  Pallas kernels  12 us (12%)
  starting transfers between devices  11.9 us (12%)
  between operations  2.04 us (2%)
    unnamed x62, local copies, waits for them, and re-layouts  24.9 us
    all_to_all x2, waiting for transfers between devices, exchange(): lax.all_to_all(blocks, 'tensor', split_axis=0, concat_axis=0, tiled=True)  20.7 us
    all_to_all x2, blocking collectives, exchange(): lax.all_to_all(blocks, 'tensor', split_axis=0, concat_axis=0, tiled=True)  18.3 us
    pallas_call x7, Pallas kernels, call(): pl.pallas_call(kernel, out_shape=outs, in_specs=[pl.BlockSpec(memory_spac...  12 us
    ppermute x7, waiting for transfers between devices, hop(): lax.ppermute(value, 'tensor', [(i, i ^ step) for i in range(devices)])  7.26 us
    all_to_all x2, starting transfers between devices, exchange(): lax.all_to_all(blocks, 'tensor', split_axis=0, concat_axis=0, tiled=True)  7.14 us
    ppermute x7, starting transfers between devices, hop(): lax.ppermute(value, 'tensor', [(i, i ^ step) for i in range(devices)])  4.74 us
  transfers between devices with their start and end apart: 9, of which 6 were waited for; matrix products, arithmetic and copies ran while one was open for 0% of the time, Pallas kernels for 2%

profile of v1, /device:TPU:0, one launch (start us, length us, event | category | flops | bytes accessed | tf_op | source)
XLA Modules:
  0.0 97.1 jit_solution(8499004764879162049)
XLA Ops:
  0.0 3.9 %collective-permute-start.5 = (bf16[32,2048]{1,0:T(8,128)(2,1)}, bf16[32,2048]{1,0:T(8,128)(2,1)S(1)}, u32[]{:S(2)}, u32[]{:S(2)}) collective-permute-start(bf16[32,2048]{1,0:T(8,128)(2,1)} %own_ref.1), channel_id=1, source_target_pairs={{0,6},{1,7},{2,4},{3,5},{4,2},{5,3},{6,0},{7,1},{8,14},{9,15},{10,... | collective-permute-start | bytes 393224 | tf_op jit(solution)/shard_map/ppermute | solution.py:58
  4.5 3.6 %collective-permute-done.5.refs_6_ = bf16[32,2048]{1,0:T(8,128)(2,1)S(1)} collective-permute-done((bf16[32,2048]{1,0:T(8,128)(2,1)}, bf16[32,2048]{1,0:T(8,128)(2,1)S(1)}, u32[]{:S(2)}, u32[]{:S(2)}) %collective-permute-start.5) | collective-permute-done | bytes 131104 | tf_op jit(solution)/shard_map/ppermute | solution.py:58
  8.1 2.3 %collective-permute-done.3.refs_4_ = bf16[32,2048]{1,0:T(8,128)(2,1)S(1)} collective-permute-done((bf16[32,2048]{1,0:T(8,128)(2,1)}, bf16[32,2048]{1,0:T(8,128)(2,1)S(1)}, u32[]{:S(2)}, u32[]{:S(2)}) %collective-permute-start.3) | collective-permute-done | bytes 131104 | tf_op jit(solution)/shard_map/ppermute | solution.py:58
  10.9 0.8 collective-permute-done.4.refs_5_
  12.0 1.6 %copy-done.3 = bf16[2048,512]{1,0:T(8,128)(2,1)S(1)} copy-done((bf16[2048,512]{1,0:T(8,128)(2,1)S(1)}, bf16[2048,512]{1,0:T(8,128)(2,1)}, u32[]{:S(2)}) %copy-start.3) | copy-done | bytes 2097176
  13.6 0.9 copy-done.11
  14.5 1.0 %copy-done.13 = bf16[128,2048]{1,0:T(8,128)(2,1)S(1)} copy-done((bf16[128,2048]{1,0:T(8,128)(2,1)S(1)}, bf16[128,2048]{1,0:T(8,128)(2,1)}, u32[]{:S(2)}) %copy-start.13) | copy-done | bytes 524312
  15.6 0.7 copy-done.20
  16.2 2.3 %project.1 = (bf16[8,32,640]{2,1,0:T(8,128)(2,1)}, bf16[256,2048]{1,0:T(8,128)(2,1)S(1)}) custom-call(bf16[32,2048]{1,0:T(8,128)(2,1)S(1)} %copy-done.11, bf16[32,2048]{1,0:T(8,128)(2,1)S(1)} %collective-permute-done.refs_1_, bf16[32,2048]{1,0:T(8,128)(2,1)S(1)} %collective-permute-done.1.refs_2_, bf16[32,2048]{1,0:T(8,128)(2,1)S(1)} %collective-permute-done.2.refs_3_, ...), custom_call_target="tpu_custom_call" | custom-call | flops 671088640 | bytes 2621440 | tf_op jit(solution)/shard_map/project/pallas_call | solution.py:40
  18.5 3.4 %all-to-all-start = ((bf16[8,32,640]{2,1,0:T(8,128)(2,1)}), bf16[8,32,640]{2,1,0:T(8,128)(2,1)S(1)}, u32[]{:S(2)}, u32[]{:S(2)}) async-start(bf16[8,32,640]{2,1,0:T(8,128)(2,1)} %get-tuple-element.17), calls=%async_computation | async-start | bytes 655360 | tf_op jit(solution)/shard_map/all_to_all | solution.py:53
  23.9 1.2 %copy-done.5 = bf16[1,1024,512]{2,1,0:T(8,128)(2,1)S(1)} copy-done((bf16[1,1024,512]{2,1,0:T(8,128)(2,1)S(1)}, bf16[1,1024,512]{2,1,0:T(8,128)(2,1)}, u32[]{:S(2)}) %copy-start.5) | copy-done | bytes 1048600
  25.1 1.2 %copy-done.6 = bf16[1,1024,512]{2,1,0:T(8,128)(2,1)S(1)} copy-done((bf16[1,1024,512]{2,1,0:T(8,128)(2,1)S(1)}, bf16[1,1024,512]{2,1,0:T(8,128)(2,1)}, u32[]{:S(2)}) %copy-start.6) | copy-done | bytes 1048600
  26.4 0.7 copy-done.21
  27.1 0.7 copy-done.22
  29.7 1.8 %prep.1 = (bf16[640,512]{1,0:T(8,128)(2,1)S(1)}, bf16[640,512]{1,0:T(8,128)(2,1)S(1)}, f32[32,640]{1,0:T(8,128)S(1)}, f32[32,128]{1,0:T(8,128)S(1)}, f32[32,128]...) custom-call(bf16[1,1024,512]{2,1,0:T(8,128)(2,1)S(1)} %copy-done.5, ...), custom_call_target="tpu_custom_call" | custom-call | bytes 2621440 | tf_op jit(solution)/shard_map/prep/pallas_call | solution.py:40
  31.5 0.8 copy-done.7
  32.3 0.9 copy-done.9
  35.6 1.1 %copy-done.8 = bf16[640,512]{1,0:T(8,128)(2,1)S(1)} copy-done((bf16[640,512]{1,0:T(8,128)(2,1)S(1)}, bf16[640,512]{1,0:T(8,128)(2,1)}, u32[]{:S(2)}) %copy-start.8) | copy-done | bytes 655384
  36.7 1.1 %copy-done.10 = bf16[640,512]{1,0:T(8,128)(2,1)S(1)} copy-done((bf16[640,512]{1,0:T(8,128)(2,1)S(1)}, bf16[640,512]{1,0:T(8,128)(2,1)}, u32[]{:S(2)}) %copy-start.10) | copy-done | bytes 655384
  37.8 0.9 copy-done.15
  38.7 0.7 copy-done.17
  40.7 2.2 %attend.1 = bf16[8,32,512]{2,1,0:T(8,128)(2,1)S(1)} custom-call(bf16[8,32,640]{2,1,0:T(8,128)(2,1)S(1)} %all-to-all-done.got_ref, f32[1,128]{1,0:T(1,128)S(1)} %bitcast.10, f32[1,128]{1,0:T(1,128)S(1)} %bitcast.11, bf16[640,512]{1,0:T(8,128)(2,1)S(1)} %copy-done.8, bf16[640,512]{1,0:T(8,128)(2,1)S(1)} %copy-done.10, f32[32,640]{1,0:T(8,128)S(1)} %copy-done.15, ...), custom_call_target="tpu_custom_call" | custom-call | flops 335544320 | bytes 1310720 | tf_op jit(solution)/shard_map/attend/pallas_call | solution.py:40
  42.9 10.9 %all_to_all.20.got_ref = bf16[8,32,512]{2,1,0:T(8,128)(2,1)S(1)} all-to-all(bf16[8,32,512]{2,1,0:T(8,128)(2,1)S(1)} %attend.1), channel_id=1, replica_groups=mesh['group'=4,'tensor'=8] {'tensor'}, dimensions={0} | all-to-all | bytes 524288 | tf_op jit(solution)/shard_map/all_to_all | solution.py:53
  53.8 2.3 %spread.1 = bf16[8,48,2048]{2,1,0:T(8,128)(2,1)} custom-call(bf16[8,32,512]{2,1,0:T(8,128)(2,1)S(1)} %all_to_all.20.got_ref, bf16[128,256]{1,0:T(8,128)(2,1)S(1)} %get-tuple-element.23.pick_ref, bf16[512,2048]{1,0:T(8,128)(2,1)S(1)} %copy-done.4), custom_call_target="tpu_custom_call" | custom-call | flops 805306368 | bytes 2097152 | tf_op jit(solution)/shard_map/spread/pallas_call | solution.py:40
  56.0 3.7 %all-to-all-start.2 = ((bf16[8,48,2048]{2,1,0:T(8,128)(2,1)}), bf16[8,48,2048]{2,1,0:T(8,128)(2,1)S(1)}, u32[]{:S(2)}, u32[]{:S(2)}) async-start(bf16[8,48,2048]{2,1,0:T(8,128)(2,1)} %spread.1), calls=%async_computation.2 | async-start | bytes 3145728 | tf_op jit(solution)/shard_map/all_to_all | solution.py:53
  60.0 20.7 %all-to-all-done.2.got_ref = bf16[8,48,2048]{2,1,0:T(8,128)(2,1)S(1)} async-done(((bf16[8,48,2048]{2,1,0:T(8,128)(2,1)}), bf16[8,48,2048]{2,1,0:T(8,128)(2,1)S(1)}, u32[]{:S(2)}, u32[]{:S(2)}) %all-to-all-start.2) | async-done | bytes 1572896 | tf_op jit(solution)/shard_map/all_to_all | solution.py:53
  80.7 1.9 %copy-done = bf16[1,768,2048]{2,1,0:T(8,128)(2,1)S(1)} copy-done((bf16[1,768,2048]{2,1,0:T(8,128)(2,1)S(1)}, bf16[1,768,2048]{2,1,0:T(8,128)(2,1)}, u32[]{:S(2)}) %copy-start) | copy-done | bytes 3145752
  82.6 1.9 %copy-done.1 = bf16[1,768,2048]{2,1,0:T(8,128)(2,1)S(1)} copy-done((bf16[1,768,2048]{2,1,0:T(8,128)(2,1)S(1)}, bf16[1,768,2048]{2,1,0:T(8,128)(2,1)}, u32[]{:S(2)}) %copy-start.1) | copy-done | bytes 3145752
  84.5 1.9 %copy-done.2 = bf16[1,768,2048]{2,1,0:T(8,128)(2,1)S(1)} copy-done((bf16[1,768,2048]{2,1,0:T(8,128)(2,1)S(1)}, bf16[1,768,2048]{2,1,0:T(8,128)(2,1)}, u32[]{:S(2)}) %copy-start.2) | copy-done | bytes 3145752
  86.4 2.5 %expert.1 = (bf16[8,2,2048]{2,1,0:T(2,128)(2,1)S(1)}, f32[32,2048]{1,0:T(8,128)S(1)}) custom-call(bf16[8,48,2048]{2,1,0:T(8,128)(2,1)S(1)} %all-to-all-done.2.got_ref, bf16[32,2048]{1,0:T(8,128)(2,1)S(1)} %copy-done.12, f32[16,2048]{1,0:T(8,128)S(1)} %select.1.picked_ref, f32[1,2048]{1,0:T(1,128)S(1)} %bitcast.9, f32[16,128]{1,0:T(8,128)S(1)} %copy-done.25, ...), custom_call_target="tpu_custom_call" | custom-call | flops 150994944 | bytes 9437184 | tf_op jit(solution)/shard_map/expert/pallas_call | solution.py:40
  88.9 7.4 %all_to_all.21.got_ref = bf16[8,2,2048]{2,1,0:T(2,128)(2,1)S(1)} all-to-all(bf16[8,2,2048]{2,1,0:T(2,128)(2,1)S(1)} %get-tuple-element.27), channel_id=1, replica_groups=mesh['group'=4,'tensor'=8] {'tensor'}, dimensions={0} | all-to-all | bytes 131072 | tf_op jit(solution)/shard_map/all_to_all | solution.py:53
  96.3 0.9 combine.1
  (57 shorter events, 7.3 us)
Async XLA Ops:
  0.0 8.1 %collective-permute-start.5 = (bf16[32,2048]{1,0:T(8,128)(2,1)}, bf16[32,2048]{1,0:T(8,128)(2,1)S(1)}, u32[]{:S(2)}, u32[]{:S(2)}) collective-permute-start(bf16[32,2048]{1,0:T(8,128)(2,1)} %own_ref.1), channel_id=1, source_target_pairs={{0,6},{1,7},{2,4},{3,5},{4,2},{5,3},{6,0},{7,1},{8,14},{9,15},{10,... | collective-permute-start | bytes 393224 | tf_op jit(solution)/shard_map/ppermute | solution.py:58
  3.9 6.5 %collective-permute-start.3 = (bf16[32,2048]{1,0:T(8,128)(2,1)}, bf16[32,2048]{1,0:T(8,128)(2,1)S(1)}, u32[]{:S(2)}, u32[]{:S(2)}) collective-permute-start(bf16[32,2048]{1,0:T(8,128)(2,1)} %own_ref.1), channel_id=1, source_target_pairs={{0,4},{1,5},{2,6},{3,7},{4,0},{5,1},{6,2},{7,3},{8,12},{9,13},{10,... | collective-permute-start | bytes 393224 | tf_op jit(solution)/shard_map/ppermute | solution.py:58
  4.4 6.3 %collective-permute-start.1 = (bf16[32,2048]{1,0:T(8,128)(2,1)}, bf16[32,2048]{1,0:T(8,128)(2,1)S(1)}, u32[]{:S(2)}, u32[]{:S(2)}) collective-permute-start(bf16[32,2048]{1,0:T(8,128)(2,1)} %own_ref.1), channel_id=1, source_target_pairs={{0,2},{1,3},{2,0},{3,1},{4,6},{5,7},{6,4},{7,5},{8,10},{9,11},{10,... | collective-permute-start | bytes 393224 | tf_op jit(solution)/shard_map/ppermute | solution.py:58
  4.5 6.5 %collective-permute-start = (bf16[32,2048]{1,0:T(8,128)(2,1)}, bf16[32,2048]{1,0:T(8,128)(2,1)S(1)}, u32[]{:S(2)}, u32[]{:S(2)}) collective-permute-start(bf16[32,2048]{1,0:T(8,128)(2,1)} %own_ref.1), channel_id=1, source_target_pairs={{0,1},{1,0},{2,3},{3,2},{4,5},{5,4},{6,7},{7,6},{8,9},{9,8},{10,11... | collective-permute-start | bytes 393224 | tf_op jit(solution)/shard_map/ppermute | solution.py:58
  8.1 2.8 %collective-permute-start.6 = (bf16[32,2048]{1,0:T(8,128)(2,1)S(1)}, bf16[32,2048]{1,0:T(8,128)(2,1)S(1)}, u32[]{:S(2)}, u32[]{:S(2)}) collective-permute-start(bf16[32,2048]{1,0:T(8,128)(2,1)S(1)} %collective-permute-done.5.refs_6_), channel_id=1, source_target_pairs={{0,1},{1,0},{2,3},{3,2},{4,5},{5,4},{6,7},{7,6},{8,9},{9,8},{10,11... | collective-permute-start | bytes 393224 | tf_op jit(solution)/shard_map/ppermute | solution.py:58
  10.4 1.3 %collective-permute-start.4 = (bf16[32,2048]{1,0:T(8,128)(2,1)S(1)}, bf16[32,2048]{1,0:T(8,128)(2,1)S(1)}, u32[]{:S(2)}, u32[]{:S(2)}) collective-permute-start(bf16[32,2048]{1,0:T(8,128)(2,1)S(1)} %collective-permute-done.3.refs_4_), channel_id=1, source_target_pairs={{0,1},{1,0},{2,3},{3,2},{4,5},{5,4},{6,7},{7,6},{8,9},{9,8},{10,11... | collective-permute-start | bytes 393224 | tf_op jit(solution)/shard_map/ppermute | solution.py:58
  10.7 1.3 %collective-permute-start.2 = (bf16[32,2048]{1,0:T(8,128)(2,1)S(1)}, bf16[32,2048]{1,0:T(8,128)(2,1)S(1)}, u32[]{:S(2)}, u32[]{:S(2)}) collective-permute-start(bf16[32,2048]{1,0:T(8,128)(2,1)S(1)} %collective-permute-done.1.refs_2_), channel_id=1, source_target_pairs={{0,1},{1,0},{2,3},{3,2},{4,5},{5,4},{6,7},{7,6},{8,9},{9,8},{10,11... | collective-permute-start | bytes 393224 | tf_op jit(solution)/shard_map/ppermute | solution.py:58
  12.0 1.6 %copy-start.3 = (bf16[2048,512]{1,0:T(8,128)(2,1)S(1)}, bf16[2048,512]{1,0:T(8,128)(2,1)}, u32[]{:S(2)}) copy-start(bf16[2048,512]{1,0:T(8,128)(2,1)} %refs_9_.1) | copy-start | bytes 6291460
  13.6 0.9 copy-start.11
  14.5 1.0 %copy-start.13 = (bf16[128,2048]{1,0:T(8,128)(2,1)S(1)}, bf16[128,2048]{1,0:T(8,128)(2,1)}, u32[]{:S(2)}) copy-start(bf16[128,2048]{1,0:T(8,128)(2,1)} %refs_10_.1) | copy-start | bytes 1572868
  15.5 0.7 copy-start.20
  18.5 17.1 %all-to-all-start = ((bf16[8,32,640]{2,1,0:T(8,128)(2,1)}), bf16[8,32,640]{2,1,0:T(8,128)(2,1)S(1)}, u32[]{:S(2)}, u32[]{:S(2)}) async-start(bf16[8,32,640]{2,1,0:T(8,128)(2,1)} %get-tuple-element.17), calls=%async_computation | async-start | bytes 655360 | tf_op jit(solution)/shard_map/all_to_all | solution.py:53
  23.9 1.2 %copy-start.5 = (bf16[1,1024,512]{2,1,0:T(8,128)(2,1)S(1)}, bf16[1,1024,512]{2,1,0:T(8,128)(2,1)}, u32[]{:S(2)}) copy-start(bf16[1,1024,512]{2,1,0:T(8,128)(2,1)} %key_cache.1) | copy-start | bytes 3145732
  25.1 1.2 %copy-start.6 = (bf16[1,1024,512]{2,1,0:T(8,128)(2,1)S(1)}, bf16[1,1024,512]{2,1,0:T(8,128)(2,1)}, u32[]{:S(2)}) copy-start(bf16[1,1024,512]{2,1,0:T(8,128)(2,1)} %value_cache.1) | copy-start | bytes 3145732
  26.4 0.7 copy-start.21
  27.1 0.7 copy-start.22
  27.8 0.7 copy-start.26
  29.7 24.0 %copy-start.4 = (bf16[512,2048]{1,0:T(8,128)(2,1)S(1)}, bf16[512,2048]{1,0:T(8,128)(2,1)}, u32[]{:S(2)}) copy-start(bf16[512,2048]{1,0:T(8,128)(2,1)} %w_ref.1) | copy-start | bytes 6291460
  31.5 0.8 copy-start.7
  32.3 0.9 copy-start.9
  35.6 1.1 %copy-start.8 = (bf16[640,512]{1,0:T(8,128)(2,1)S(1)}, bf16[640,512]{1,0:T(8,128)(2,1)}, u32[]{:S(2)}) copy-start(bf16[640,512]{1,0:T(8,128)(2,1)} %copy-done.7) | copy-start | bytes 1966084
  36.7 1.1 %copy-start.10 = (bf16[640,512]{1,0:T(8,128)(2,1)S(1)}, bf16[640,512]{1,0:T(8,128)(2,1)}, u32[]{:S(2)}) copy-start(bf16[640,512]{1,0:T(8,128)(2,1)} %copy-done.9) | copy-start | bytes 1966084
  37.8 0.9 copy-start.15
  38.7 0.7 copy-start.17
  56.0 24.7 %copy-start.12 = (bf16[32,2048]{1,0:T(8,128)(2,1)S(1)}, bf16[32,2048]{1,0:T(8,128)(2,1)}, u32[]{:S(2)}) copy-start(bf16[32,2048]{1,0:T(8,128)(2,1)} %own_ref.1) | copy-start | bytes 393220
  56.0 24.7 %copy-start.23 = (f32[2048]{0:T(1024)S(1)}, f32[2048]{0:T(1024)}, u32[]{:S(2)}) copy-start(f32[2048]{0:T(1024)} %param.28) | copy-start | bytes 24580
  56.0 24.7 %copy-start.25 = (f32[16,128]{1,0:T(8,128)S(1)}, f32[16,128]{1,0:T(8,128)}, u32[]{:S(2)}) copy-start(f32[16,128]{1,0:T(8,128)} %copy-done.24) | copy-start | bytes 24580
  56.0 24.7 %all-to-all-start.2 = ((bf16[8,48,2048]{2,1,0:T(8,128)(2,1)}), bf16[8,48,2048]{2,1,0:T(8,128)(2,1)S(1)}, u32[]{:S(2)}, u32[]{:S(2)}) async-start(bf16[8,48,2048]{2,1,0:T(8,128)(2,1)} %spread.1), calls=%async_computation.2 | async-start | bytes 3145728 | tf_op jit(solution)/shard_map/all_to_all | solution.py:53
  80.7 1.9 %copy-start = (bf16[1,768,2048]{2,1,0:T(8,128)(2,1)S(1)}, bf16[1,768,2048]{2,1,0:T(8,128)(2,1)}, u32[]{:S(2)}) copy-start(bf16[1,768,2048]{2,1,0:T(8,128)(2,1)} %wg_ref.1) | copy-start | bytes 9437188
  82.6 1.9 %copy-start.1 = (bf16[1,768,2048]{2,1,0:T(8,128)(2,1)S(1)}, bf16[1,768,2048]{2,1,0:T(8,128)(2,1)}, u32[]{:S(2)}) copy-start(bf16[1,768,2048]{2,1,0:T(8,128)(2,1)} %wu_ref.1) | copy-start | bytes 9437188
  84.5 1.9 %copy-start.2 = (bf16[1,768,2048]{2,1,0:T(8,128)(2,1)S(1)}, bf16[1,768,2048]{2,1,0:T(8,128)(2,1)}, u32[]{:S(2)}) copy-start(bf16[1,768,2048]{2,1,0:T(8,128)(2,1)} %wd_ref.1) | copy-start | bytes 9437188
  86.4 9.9 %copy-start.19 = (f32[32,16]{1,0:T(8,128)S(1)}, f32[32,16]{1,0:T(8,128)}, u32[]{:S(2)}) copy-start(f32[32,16]{1,0:T(8,128)} %copy-done.18) | copy-start | bytes 6148
  (8 other events, 5.0 us)
